TPU v7x, 32 devices: a whole 2x2x4 slice. The times are simulated.
32 devices in a mesh: tm: 8 (over z, core), space: 4 (over y, x).
Axes of the slice: x: 2, y: 2, z: 4, core: 2. Of those that a mesh axis runs over, the one named last changes fastest.
Arguments:
- increment: float32 [8, 4, 137, 512], P('tm', None, None, 'space'), may hold values from -26 to 26
- courant: float32 [8, 4, 137, 512], P('tm', None, None, 'space'), may hold values from -0.9 to 0.9
- error_weight: float32 [4, 137], replicated, may hold values from 0.5 to 2
- obs_code: int32 [8, 4, 4, 128], P('tm', 'space'), may hold values from 0 to 280574, as said below
- obs_values: float32 [8, 4, 4, 3, 128], P('tm', 'space'), as said below
- obs_count: int32 [8, 4, 4], P('tm', 'space'), may hold values from 25 to 128, as said below
Outputs:
- new_increment: float32 [8, 4, 137, 512], P('tm', None, None, 'space')
- departures: float32 [8, 4, 4, 128], P('tm', 'space')
Inputs may be any that keep to these rules, and one draw needn't show every extreme that they name: `obs_code`: code = ((t * 4 + f) * 137 + l) * 128 + c for an observation of the state after step t + 1 of its sub-window, field f, level l, between columns c and c + 1 of the destination tile, c < 127; slots at or beyond the count carry no observation. `obs_values`: row 1 lies in [0, 1], row 2 in [0.5, 4]. `obs_count`: in every sub-window some destination tile receives 128 observations from every source tile.
All inputs are finite; a program needn't handle non-finite values.
Results may differ from a plain program's by a relative error of at most 0.0003.
Values sent between devices are 32-bit elements; how exact they have to be, the bound alone decides.
A program may use at most 64 MiB of HBM per device.

v0:
```python
import jax
import jax.numpy as jnp
from jax import lax
from jax.sharding import PartitionSpec as P


def padded_2(array, sides, width):
    for axis, dim in sides:
        size, length = (lax.axis_size(axis), array.shape[dim])
        up = [(i, (i + 1) % size) for i in range(size)]
        down = [(j, i) for i, j in up]
        last = lax.slice_in_dim(array, length - width, length, axis=dim)
        initial = lax.slice_in_dim(array, 0, width, axis=dim)
        before = lax.ppermute(last, axis, up)
        after = lax.ppermute(initial, axis, down)
        array = jnp.concatenate([before, array, after], axis=dim)
    return array


def passed_along(array, axis, by):
    size = lax.axis_size(axis)
    pairs = [(i, i + by) for i in range(size) if 0 <= i + by < size]
    return lax.ppermute(array, axis, pairs)


def on_device(increment, courant, error_weight, obs_code, obs_values, obs_count):
    start = increment[0]
    cour = courant[0]
    steps = cour.shape[0]
    per_state = start.size
    slots = obs_code.shape[-1]
    qinv = error_weight[:, :, None]
    code_in, values_in, count_in = (
        lax.all_to_all(obs_code, "space", split_axis=2, concat_axis=2, tiled=True),
        lax.all_to_all(obs_values, "space", split_axis=2, concat_axis=2, tiled=True),
        lax.all_to_all(obs_count, "space", split_axis=2, concat_axis=2, tiled=True),
    )
    code_in = code_in[0, 0]
    values_in = values_in[0, 0]
    flat = code_in % per_state
    when = code_in // per_state
    valid = jnp.arange(slots, dtype=jnp.int32)[None, :] < count_in[0, 0][:, None]
    innovation = values_in[:, 0, :]
    weight = values_in[:, 1, :]
    rinv = values_in[:, 2, :]
    margin = 1
    cour_pad = padded_2(cour, (("space", 2),), margin)
    left_pad = 0.5 * cour_pad * (1.0 + cour_pad)
    right_pad = 0.5 * cour_pad * (cour_pad - 1.0)
    centre = 1.0 - cour * cour
    seen_all = jnp.zeros(flat.shape, jnp.float32)
    left = left_pad[:, :, 1:-1]
    right = right_pad[:, :, 1:-1]
    state = start
    for step in range(steps):
        padded = padded_2(state, (("space", 2),), 1)
        state = (
            centre[step] * state + left[step] * padded[:, :, :-2] + right[step] * padded[:, :, 2:]
        )
        line = state.reshape(-1)
        seen = weight * line[flat] + (1.0 - weight) * line[flat + 1]
        seen_all = jnp.where(when == step, seen, seen_all)
    departed = jnp.where(valid, seen_all - innovation, 0.0)
    pushed = rinv * departed
    previous = passed_along(state, "tm", 1)
    jump_own = start - previous
    weighted_own = qinv * jump_own
    weighted_next = passed_along(weighted_own, "tm", -1)
    jump_part = jnp.sum(weighted_own * jump_own)
    target = when * per_state + flat
    forcing = jnp.zeros((steps * per_state,), jnp.float32)
    forcing = forcing.at[target].add(weight * pushed).at[target + 1].add((1.0 - weight) * pushed)
    forcing = forcing.reshape((steps,) + start.shape)
    lam = -weighted_next + forcing[steps - 1]
    for step in reversed(range(steps)):
        retreat_padded = padded_2(lam, (("space", 2),), 1)
        lam = (
            centre[step] * lam
            + left_pad[step][:, 2:] * retreat_padded[:, :, 2:]
            + right_pad[step][:, :-2] * retreat_padded[:, :, :-2]
        )
        if step > 0:
            lam = lam + forcing[step - 1]
    gradient = weighted_own + lam
    cost_part = 0.5 * (jump_part + jnp.sum(pushed * departed))
    norm_part = jnp.sum(gradient * gradient)
    cost, norm = lax.psum((cost_part, norm_part), ("tm", "space"))
    renewed = increment - cost / norm * gradient[None]
    returned = lax.all_to_all(
        departed[None, None], "space", split_axis=2, concat_axis=2, tiled=True
    )
    return (renewed, returned)


def solution(mesh):
    in_specs = (
        P("tm", None, None, "space"),
        P("tm", None, None, "space"),
        P(),
        P("tm", "space", None, None),
        P("tm", "space", None, None, None),
        P("tm", "space", None),
    )
    out_specs = (P("tm", None, None, "space"), P("tm", "space", None, None))
    return jax.shard_map(
        on_device, mesh=mesh, in_specs=in_specs, out_specs=out_specs, check_vma=False
    )
```

profile of v0, /device:TPU:0, one launch (start us, length us, event | category | flops | bytes accessed | tf_op | source)
XLA Modules:
  0.0 220.6 jit_solution(10533462246855914328)
XLA Ops:
  0.6 1.3 copy.83
  1.9 5.2 %all-to-all-start.1 = ((s32[1,1,4]{1,0,2:T(1,128)}), s32[1,1,4]{1,0,2:T(1,128)S(1)}, u32[]{:S(2)}, u32[]{:S(2)}) async-start(s32[1,1,4]{1,0,2:T(1,128)} %copy.83), calls=%async_computation.1 | async-start | bytes 4096 | tf_op jit(solution)/shard_map/all_to_all | solution.py:36
  7.1 1.2 copy.68
  8.3 2.1 collective-permute-start
  13.2 1.1 collective-permute-start.2
  14.3 1.9 collective-permute-start.3
  16.2 3.2 %all-to-all-start.2 = ((s32[1,1,4,128]{3,1,0,2:T(1,128)}), s32[1,1,4,128]{3,1,0,2:T(1,128)S(1)}, u32[]{:S(2)}, u32[]{:S(2)}) async-start(s32[1,1,4,128]{3,1,0,2:T(1,128)} %bitcast.16), calls=%async_computation.2 | async-start | bytes 4096 | tf_op jit(solution)/shard_map/all_to_all | solution.py:34
  20.7 8.2 %all-to-all-done.2 = s32[1,1,4,128]{3,1,0,2:T(1,128)S(1)} async-done(((s32[1,1,4,128]{3,1,0,2:T(1,128)}), s32[1,1,4,128]{3,1,0,2:T(1,128)S(1)}, u32[]{:S(2)}, u32[]{:S(2)}) %all-to-all-start.2) | async-done | bytes 2080 | tf_op jit(solution)/shard_map/all_to_all | solution.py:34
  28.9 3.2 %all-to-all-start = ((f32[1,1,4,3,128]{4,3,1,0,2:T(4,128)}), f32[1,1,4,3,128]{4,3,1,0,2:T(4,128)S(1)}, u32[]{:S(2)}, u32[]{:S(2)}) async-start(f32[1,1,4,3,128]{4,3,1,0,2:T(4,128)} %copy.81), calls=%async_computation | async-start | bytes 16384 | tf_op jit(solution)/shard_map/all_to_all | solution.py:35
  32.7 1.3 fusion.35
  34.1 2.0 collective-permute-start.4
  37.3 7.6 %collective-permute-done.4 = f32[4,137,1]{2,1,0:T(8,128)S(1)} collective-permute-done((f32[4,137,1]{2,1,0:T(8,128)S(1)}, f32[4,137,1]{2,1,0:T(8,128)S(1)}, u32[]{:S(2)}, u32[]{:S(2)}) %collective-permute-start.4) | collective-permute-done | bytes 2224 | tf_op jit(solution)/shard_map/ppermute | solution.py:14
  44.9 3.5 %collective-permute-done.5 = f32[4,137,1]{2,1,0:T(8,128)} collective-permute-done((f32[4,137,1]{2,1,0:T(8,128)S(1)}, f32[4,137,1]{2,1,0:T(8,128)}, u32[]{:S(2)}, u32[]{:S(2)}) %collective-permute-start.5) | collective-permute-done | bytes 2224 | tf_op jit(solution)/shard_map/ppermute | solution.py:15
  48.4 1.3 fusion.31
  50.6 1.5 collective-permute-start.6
  52.1 1.5 collective-permute-start.7
  54.0 3.1 %gather_fusion.7 = f32[512]{0:T(512)S(1)} fusion(f32[70144]{0:T(1024)S(1)} %reshape.355, s32[1024]{0:T(1024)S(1)} %get-tuple-element.72), kind=kCustom, calls=%fused_computation.7 | custom fusion | bytes 6144 | tf_op jit(solution)/shard_map/gather | solution.py:61
  57.1 3.1 %gather_fusion.6 = f32[512]{0:T(512)S(1)} fusion(f32[70144]{0:T(1024)S(1)} %reshape.355, s32[1024]{0:T(1024)S(1)} %get-tuple-element.73), kind=kCustom, calls=%fused_computation.6 | custom fusion | bytes 6144 | tf_op jit(solution)/shard_map/gather | solution.py:61
  60.3 3.1 %gather_fusion.5 = f32[512]{0:T(512)S(1)} fusion(f32[70144]{0:T(1024)S(1)} %reshape.354, s32[1024]{0:T(1024)S(1)} %get-tuple-element.72), kind=kCustom, calls=%fused_computation.5 | custom fusion | bytes 6144 | tf_op jit(solution)/shard_map/gather | solution.py:61
  63.5 3.1 %gather_fusion.4 = f32[512]{0:T(512)S(1)} fusion(f32[70144]{0:T(1024)S(1)} %reshape.354, s32[1024]{0:T(1024)S(1)} %get-tuple-element.73), kind=kCustom, calls=%fused_computation.4 | custom fusion | bytes 6144 | tf_op jit(solution)/shard_map/gather | solution.py:61
  66.6 1.3 fusion.27
  68.7 2.4 %collective-permute-start.9 = (f32[4,137,1]{2,1,0:T(8,128)S(1)}, f32[4,137,1]{2,1,0:T(8,128)S(1)}, u32[]{:S(2)}, u32[]{:S(2)}) collective-permute-start(f32[4,137,1]{2,1,0:T(8,128)S(1)} %get-tuple-element.56), channel_id=1, source_target_pairs={{1,0},{2,1},{3,2},{0,3},{5,4},{6,5},{7,6},{4,7},{9,8},{10,9},{11,1... | collective-permute-start | bytes 6584 | tf_op jit(solution)/shard_map/ppermute | solution.py:15
  71.1 3.1 %gather_fusion.3 = f32[512]{0:T(512)S(1)} fusion(f32[70144]{0:T(1024)S(1)} %reshape.353, s32[1024]{0:T(1024)S(1)} %get-tuple-element.72), kind=kCustom, calls=%fused_computation.3 | custom fusion | bytes 6144 | tf_op jit(solution)/shard_map/gather | solution.py:61
  74.2 3.1 %gather_fusion.2 = f32[512]{0:T(512)S(1)} fusion(f32[70144]{0:T(1024)S(1)} %reshape.353, s32[1024]{0:T(1024)S(1)} %get-tuple-element.73), kind=kCustom, calls=%fused_computation.2 | custom fusion | bytes 6144 | tf_op jit(solution)/shard_map/gather | solution.py:61
  77.4 1.9 collective-permute-done.9
  79.7 3.1 %gather_fusion.1 = f32[512]{0:T(512)S(1)} fusion(f32[70144]{0:T(1024)S(1)} %reshape.352, s32[1024]{0:T(1024)S(1)} %get-tuple-element.72), kind=kCustom, calls=%fused_computation.1 | custom fusion | bytes 6144 | tf_op jit(solution)/shard_map/gather | solution.py:61
  82.8 3.1 %gather_fusion = f32[512]{0:T(512)S(1)} fusion(f32[70144]{0:T(1024)S(1)} %reshape.352, s32[1024]{0:T(1024)S(1)} %get-tuple-element.73), kind=kCustom, calls=%fused_computation | custom fusion | bytes 6144 | tf_op jit(solution)/shard_map/gather | solution.py:61
  86.0 1.3 collective-permute-start.10
  88.7 3.5 %scatter_custom_fusion = f32[280576]{0:T(1024)S(1)} fusion(s32[512]{0:T(512)S(1)} %fusion.42, f32[512]{0:T(512)S(1)} %get-tuple-element.67, f32[]{:T(128)} %constant.16.clone.1), kind=kCustom, calls=%fused_computation.10 | custom fusion | flops 512 | bytes 1122308 | tf_op jit(solution)/shard_map/scatter-add | solution.py:72
  92.2 3.7 %scatter_fusion = f32[280576]{0:T(1024)S(1)} fusion(f32[280576]{0:T(1024)S(1)} %scatter_custom_fusion, s32[512]{0:T(512)S(1)} %get-tuple-element.70, f32[512]{0:T(512)S(1)} %get-tuple-element.66), kind=kCustom, calls=%fused_computation.9 | custom fusion | flops 512 | bytes 8192 | tf_op jit(solution)/shard_map/scatter-add | solution.py:72
  96.8 1.3 collective-permute-start.11
  100.0 2.4 %collective-permute-done.11 = f32[4,137,128]{2,1,0:T(8,128)} collective-permute-done((f32[4,137,128]{2,1,0:T(8,128)}, f32[4,137,128]{2,1,0:T(8,128)}, u32[]{:S(2)}, u32[]{:S(2)}) %collective-permute-start.11) | collective-permute-done | bytes 280608 | tf_op jit(solution)/shard_map/ppermute | solution.py:23
  102.4 1.0 negate_add_fusion
  104.3 1.2 collective-permute-start.12
  108.4 3.0 %collective-permute-done.12 = f32[4,137,1]{2,1,0:T(8,128)} collective-permute-done((f32[4,137,1]{2,1,0:T(8,128)}, f32[4,137,1]{2,1,0:T(8,128)}, u32[]{:S(2)}, u32[]{:S(2)}) %collective-permute-start.12) | collective-permute-done | bytes 2224 | tf_op jit(solution)/shard_map/ppermute | solution.py:15
  111.4 6.2 %collective-permute-done.13 = f32[4,137,1]{2,1,0:T(8,128)} collective-permute-done((f32[4,137,1]{2,1,0:T(8,128)}, f32[4,137,1]{2,1,0:T(8,128)}, u32[]{:S(2)}, u32[]{:S(2)}) %collective-permute-start.13) | collective-permute-done | bytes 2224 | tf_op jit(solution)/shard_map/ppermute | solution.py:14
  117.6 1.4 fusion.19
  120.2 1.7 collective-permute-start.15
  122.2 4.7 %collective-permute-done.14 = f32[4,137,1]{2,1,0:T(8,128)S(1)} collective-permute-done((f32[4,137,1]{2,1,0:T(8,128)}, f32[4,137,1]{2,1,0:T(8,128)S(1)}, u32[]{:S(2)}, u32[]{:S(2)}) %collective-permute-start.14) | collective-permute-done | bytes 2224 | tf_op jit(solution)/shard_map/ppermute | solution.py:15
  126.9 6.5 %collective-permute-done.15 = f32[4,137,1]{2,1,0:T(8,128)} collective-permute-done((f32[4,137,1]{2,1,0:T(8,128)}, f32[4,137,1]{2,1,0:T(8,128)}, u32[]{:S(2)}, u32[]{:S(2)}) %collective-permute-start.15) | collective-permute-done | bytes 2224 | tf_op jit(solution)/shard_map/ppermute | solution.py:14
  133.4 1.3 fusion.14
  135.6 1.2 collective-permute-start.16
  137.9 5.8 %collective-permute-done.16 = f32[4,137,1]{2,1,0:T(8,128)S(1)} collective-permute-done((f32[4,137,1]{2,1,0:T(8,128)}, f32[4,137,1]{2,1,0:T(8,128)S(1)}, u32[]{:S(2)}, u32[]{:S(2)}) %collective-permute-start.16) | collective-permute-done | bytes 2224 | tf_op jit(solution)/shard_map/ppermute | solution.py:15
  143.7 7.2 %collective-permute-done.17 = f32[4,137,1]{2,1,0:T(8,128)S(1)} collective-permute-done((f32[4,137,1]{2,1,0:T(8,128)}, f32[4,137,1]{2,1,0:T(8,128)S(1)}, u32[]{:S(2)}, u32[]{:S(2)}) %collective-permute-start.17) | collective-permute-done | bytes 2224 | tf_op jit(solution)/shard_map/ppermute | solution.py:14
  151.7 1.7 collective-permute-start.19
  153.4 3.2 %all-to-all-start.3 = ((f32[1,1,4,128]{3,1,0,2:T(1,128)}), f32[1,1,4,128]{3,1,0,2:T(1,128)S(1)}, u32[]{:S(2)}, u32[]{:S(2)}) async-start(f32[1,1,4,128]{3,1,0,2:T(1,128)} %bitcast.58), calls=%async_computation.3 | async-start | bytes 4096 | tf_op jit(solution)/shard_map/all_to_all | solution.py:89
  156.9 10.0 %all-to-all-done.3 = f32[1,1,4,128]{3,1,0,2:T(1,128)S(1)} async-done(((f32[1,1,4,128]{3,1,0,2:T(1,128)}), f32[1,1,4,128]{3,1,0,2:T(1,128)S(1)}, u32[]{:S(2)}, u32[]{:S(2)}) %all-to-all-start.3) | async-done | bytes 2080 | tf_op jit(solution)/shard_map/all_to_all | solution.py:89
  169.2 48.6 %all-reduce = (f32[]{:T(128)}, f32[]{:T(128)}) all-reduce(f32[]{:T(128)S(6)} %mul.422, f32[]{:T(128)} %get-tuple-element.12), channel_id=1, replica_groups=mesh['tm'=8,'space'=4] {'tm','space'}, use_global_device_ids=true, to_apply=%region_2.3 | all-reduce | flops 2 | bytes 16 | tf_op jit(solution)/shard_map/psum | solution.py:87
  (109 shorter events, 23.0 us)
Async XLA Ops:
  1.9 14.3 %all-to-all-start.1 = ((s32[1,1,4]{1,0,2:T(1,128)}), s32[1,1,4]{1,0,2:T(1,128)S(1)}, u32[]{:S(2)}, u32[]{:S(2)}) async-start(s32[1,1,4]{1,0,2:T(1,128)} %copy.83), calls=%async_computation.1 | async-start | bytes 4096 | tf_op jit(solution)/shard_map/all_to_all | solution.py:36
  8.3 23.9 %collective-permute-start = (f32[4,137,1]{1,2,0:T(1,128)S(1)}, f32[4,137,1]{1,2,0:T(1,128)S(1)}, u32[]{:S(2)}, u32[]{:S(2)}) collective-permute-start(f32[4,137,1]{1,2,0:T(1,128)S(1)} %get-tuple-element.45), channel_id=1, source_target_pairs={{0,1},{1,2},{2,3},{3,0},{4,5},{5,6},{6,7},{7,4},{8,9},{9,10},{10,1... | collective-permute-start | bytes 6584 | tf_op jit(solution)/shard_map/ppermute | solution.py:14
  10.4 21.8 %collective-permute-start.1 = (f32[4,137,1]{1,2,0:T(1,128)S(1)}, f32[4,137,1]{1,2,0:T(1,128)S(1)}, u32[]{:S(2)}, u32[]{:S(2)}) collective-permute-start(f32[4,137,1]{1,2,0:T(1,128)S(1)} %get-tuple-element.46), channel_id=1, source_target_pairs={{1,0},{2,1},{3,2},{0,3},{5,4},{6,5},{7,6},{4,7},{9,8},{10,9},{11,1... | collective-permute-start | bytes 6584 | tf_op jit(solution)/shard_map/ppermute | solution.py:15
  13.2 6.3 %copy-start.10 = (f32[1,1,4,3,128]{4,2,3,1,0:T(4,128)S(1)}, f32[1,1,4,3,128]{4,2,3,1,0:T(4,128)}, u32[]{:S(2)}) copy-start(f32[1,1,4,3,128]{4,2,3,1,0:T(4,128)} %param.10) | copy-start | bytes 18436
  13.2 19.4 %collective-permute-start.2 = (f32[4,137,1]{2,1,0:T(8,128)}, f32[4,137,1]{2,1,0:T(8,128)S(1)}, u32[]{:S(2)}, u32[]{:S(2)}) collective-permute-start(f32[4,137,1]{2,1,0:T(8,128)} %get-tuple-element.61), channel_id=1, source_target_pairs={{0,1},{1,2},{2,3},{3,0},{4,5},{5,6},{6,7},{7,4},{8,9},{9,10},{10,1... | collective-permute-start | bytes 6584 | tf_op jit(solution)/shard_map/ppermute | solution.py:14
  14.3 18.4 %collective-permute-start.3 = (f32[4,137,1]{2,1,0:T(8,128)}, f32[4,137,1]{2,1,0:T(8,128)}, u32[]{:S(2)}, u32[]{:S(2)}) collective-permute-start(f32[4,137,1]{2,1,0:T(8,128)} %get-tuple-element.62), channel_id=1, source_target_pairs={{1,0},{2,1},{3,2},{0,3},{5,4},{6,5},{7,6},{4,7},{9,8},{10,9},{11,1... | collective-permute-start | bytes 6584 | tf_op jit(solution)/shard_map/ppermute | solution.py:15
  16.2 12.7 %all-to-all-start.2 = ((s32[1,1,4,128]{3,1,0,2:T(1,128)}), s32[1,1,4,128]{3,1,0,2:T(1,128)S(1)}, u32[]{:S(2)}, u32[]{:S(2)}) async-start(s32[1,1,4,128]{3,1,0,2:T(1,128)} %bitcast.16), calls=%async_computation.2 | async-start | bytes 4096 | tf_op jit(solution)/shard_map/all_to_all | solution.py:34
  20.2 59.1 %copy-start.4 = (f32[137,128]{1,0:T(8,128)}, f32[137,128]{1,0:T(8,128)S(1)}, u32[]{:S(2)}) copy-start(f32[137,128]{1,0:T(8,128)S(1)} %copy.69) | copy-start | bytes 210436
  20.5 46.1 %copy-start.2 = (f32[137,128]{1,0:T(8,128)}, f32[137,128]{1,0:T(8,128)S(1)}, u32[]{:S(2)}) copy-start(f32[137,128]{1,0:T(8,128)S(1)} %copy.70) | copy-start | bytes 210436
  28.9 42.1 %all-to-all-start = ((f32[1,1,4,3,128]{4,3,1,0,2:T(4,128)}), f32[1,1,4,3,128]{4,3,1,0,2:T(4,128)S(1)}, u32[]{:S(2)}, u32[]{:S(2)}) async-start(f32[1,1,4,3,128]{4,3,1,0,2:T(4,128)} %copy.81), calls=%async_computation | async-start | bytes 16384 | tf_op jit(solution)/shard_map/all_to_all | solution.py:35
  34.1 10.8 %collective-permute-start.4 = (f32[4,137,1]{2,1,0:T(8,128)S(1)}, f32[4,137,1]{2,1,0:T(8,128)S(1)}, u32[]{:S(2)}, u32[]{:S(2)}) collective-permute-start(f32[4,137,1]{2,1,0:T(8,128)S(1)} %get-tuple-element.59), channel_id=1, source_target_pairs={{0,1},{1,2},{2,3},{3,0},{4,5},{5,6},{6,7},{7,4},{8,9},{9,10},{10,1... | collective-permute-start | bytes 6584 | tf_op jit(solution)/shard_map/ppermute | solution.py:14
  36.1 12.3 %collective-permute-start.5 = (f32[4,137,1]{2,1,0:T(8,128)S(1)}, f32[4,137,1]{2,1,0:T(8,128)}, u32[]{:S(2)}, u32[]{:S(2)}) collective-permute-start(f32[4,137,1]{2,1,0:T(8,128)S(1)} %get-tuple-element.60), channel_id=1, source_target_pairs={{1,0},{2,1},{3,2},{0,3},{5,4},{6,5},{7,6},{4,7},{9,8},{10,9},{11,1... | collective-permute-start | bytes 6584 | tf_op jit(solution)/shard_map/ppermute | solution.py:15
  50.6 16.0 %collective-permute-start.6 = (f32[4,137,1]{2,1,0:T(8,128)}, f32[4,137,1]{2,1,0:T(8,128)S(1)}, u32[]{:S(2)}, u32[]{:S(2)}) collective-permute-start(f32[4,137,1]{2,1,0:T(8,128)} %get-tuple-element.57), channel_id=1, source_target_pairs={{0,1},{1,2},{2,3},{3,0},{4,5},{5,6},{6,7},{7,4},{8,9},{9,10},{10,1... | collective-permute-start | bytes 6584 | tf_op jit(solution)/shard_map/ppermute | solution.py:14
  52.1 14.5 %collective-permute-start.7 = (f32[4,137,1]{2,1,0:T(8,128)}, f32[4,137,1]{2,1,0:T(8,128)}, u32[]{:S(2)}, u32[]{:S(2)}) collective-permute-start(f32[4,137,1]{2,1,0:T(8,128)} %get-tuple-element.58), channel_id=1, source_target_pairs={{1,0},{2,1},{3,2},{0,3},{5,4},{6,5},{7,6},{4,7},{9,8},{10,9},{11,1... | collective-permute-start | bytes 6584 | tf_op jit(solution)/shard_map/ppermute | solution.py:15
  68.1 9.3 %collective-permute-start.8 = (f32[4,137,1]{2,1,0:T(8,128)S(1)}, f32[4,137,1]{2,1,0:T(8,128)S(1)}, u32[]{:S(2)}, u32[]{:S(2)}) collective-permute-start(f32[4,137,1]{2,1,0:T(8,128)S(1)} %get-tuple-element.55), channel_id=1, source_target_pairs={{0,1},{1,2},{2,3},{3,0},{4,5},{5,6},{6,7},{7,4},{8,9},{9,10},{10,1... | collective-permute-start | bytes 6584 | tf_op jit(solution)/shard_map/ppermute | solution.py:14
  68.7 10.7 %collective-permute-start.9 = (f32[4,137,1]{2,1,0:T(8,128)S(1)}, f32[4,137,1]{2,1,0:T(8,128)S(1)}, u32[]{:S(2)}, u32[]{:S(2)}) collective-permute-start(f32[4,137,1]{2,1,0:T(8,128)S(1)} %get-tuple-element.56), channel_id=1, source_target_pairs={{1,0},{2,1},{3,2},{0,3},{5,4},{6,5},{7,6},{4,7},{9,8},{10,9},{11,1... | collective-permute-start | bytes 6584 | tf_op jit(solution)/shard_map/ppermute | solution.py:15
  86.0 10.0 %collective-permute-start.10 = (f32[4,137,128]{2,1,0:T(8,128)S(1)}, f32[4,137,128]{2,1,0:T(8,128)S(1)}, u32[]{:S(2)}, u32[]{:S(2)}) collective-permute-start(f32[4,137,128]{2,1,0:T(8,128)S(1)} %fusion.23), channel_id=1, source_target_pairs={{0,4},{4,8},{8,12},{12,16},{16,20},{20,24},{24,28},{1,5},{5,9},{9,... | collective-permute-start | bytes 841736 | tf_op jit(solution)/shard_map/ppermute | solution.py:23
  92.2 3.7 %copy-start = (f32[1,4,137,128]{3,1,2,0:T(4,128)S(1)}, f32[1,4,137,128]{3,1,2,0:T(4,128)}, u32[]{:S(2)}) copy-start(f32[1,4,137,128]{3,1,2,0:T(4,128)} %param.6) | copy-start | bytes 841732
  92.2 3.7 %copy-start.9 = (f32[4,137]{1,0:T(4,128)S(1)}, f32[4,137]{1,0:T(4,128)}, u32[]{:S(2)}) copy-start(f32[4,137]{1,0:T(4,128)} %param.8) | copy-start | bytes 6580
  96.8 5.6 %collective-permute-start.11 = (f32[4,137,128]{2,1,0:T(8,128)}, f32[4,137,128]{2,1,0:T(8,128)}, u32[]{:S(2)}, u32[]{:S(2)}) collective-permute-start(f32[4,137,128]{2,1,0:T(8,128)} %broadcast_multiply_fusion), channel_id=1, source_target_pairs={{4,0},{8,4},{12,8},{16,12},{20,16},{24,20},{28,24},{5,1},{9,5},{13... | collective-permute-start | bytes 841736 | tf_op jit(solution)/shard_map/ppermute | solution.py:23
  104.3 7.0 %collective-permute-start.12 = (f32[4,137,1]{2,1,0:T(8,128)}, f32[4,137,1]{2,1,0:T(8,128)}, u32[]{:S(2)}, u32[]{:S(2)}) collective-permute-start(f32[4,137,1]{2,1,0:T(8,128)} %get-tuple-element.53), channel_id=1, source_target_pairs={{1,0},{2,1},{3,2},{0,3},{5,4},{6,5},{7,6},{4,7},{9,8},{10,9},{11,1... | collective-permute-start | bytes 6584 | tf_op jit(solution)/shard_map/ppermute | solution.py:15
  105.6 2.8 %copy-start.1 = (f32[70144]{0:T(1024)S(1)}, f32[70144]{0:T(1024)}, u32[]{:S(2)}) copy-start(f32[70144]{0:T(1024)} %get-tuple-element.21) | copy-start | bytes 841732
  105.6 12.0 %collective-permute-start.13 = (f32[4,137,1]{2,1,0:T(8,128)}, f32[4,137,1]{2,1,0:T(8,128)}, u32[]{:S(2)}, u32[]{:S(2)}) collective-permute-start(f32[4,137,1]{2,1,0:T(8,128)} %get-tuple-element.54), channel_id=1, source_target_pairs={{0,1},{1,2},{2,3},{3,0},{4,5},{5,6},{6,7},{7,4},{8,9},{9,10},{10,1... | collective-permute-start | bytes 6584 | tf_op jit(solution)/shard_map/ppermute | solution.py:14
  107.2 10.4 %copy-start.5 = (f32[137,128]{1,0:T(8,128)S(1)}, f32[137,128]{1,0:T(8,128)}, u32[]{:S(2)}) copy-start(f32[137,128]{1,0:T(8,128)} %copy-done.4) | copy-start | bytes 210436
  108.4 13.5 %copy-start.8 = (f32[137,130]{0,1:T(8,128)S(1)}, f32[137,130]{0,1:T(8,128)}, u32[]{:S(2)}) copy-start(f32[137,130]{0,1:T(8,128)} %get-tuple-element.29) | copy-start | bytes 213724
  119.0 3.1 %copy-start.7 = (f32[137,130]{0,1:T(8,128)S(1)}, f32[137,130]{0,1:T(8,128)}, u32[]{:S(2)}) copy-start(f32[137,130]{0,1:T(8,128)} %get-tuple-element.75) | copy-start | bytes 213724
  119.0 14.4 %copy-start.3 = (f32[137,128]{1,0:T(8,128)S(1)}, f32[137,128]{1,0:T(8,128)}, u32[]{:S(2)}) copy-start(f32[137,128]{1,0:T(8,128)} %copy-done.2) | copy-start | bytes 210436
  119.9 7.0 %collective-permute-start.14 = (f32[4,137,1]{2,1,0:T(8,128)}, f32[4,137,1]{2,1,0:T(8,128)S(1)}, u32[]{:S(2)}, u32[]{:S(2)}) collective-permute-start(f32[4,137,1]{2,1,0:T(8,128)} %get-tuple-element.51), channel_id=1, source_target_pairs={{1,0},{2,1},{3,2},{0,3},{5,4},{6,5},{7,6},{4,7},{9,8},{10,9},{11,1... | collective-permute-start | bytes 6584 | tf_op jit(solution)/shard_map/ppermute | solution.py:15
  120.2 13.2 %collective-permute-start.15 = (f32[4,137,1]{2,1,0:T(8,128)}, f32[4,137,1]{2,1,0:T(8,128)}, u32[]{:S(2)}, u32[]{:S(2)}) collective-permute-start(f32[4,137,1]{2,1,0:T(8,128)} %get-tuple-element.52), channel_id=1, source_target_pairs={{0,1},{1,2},{2,3},{3,0},{4,5},{5,6},{6,7},{7,4},{8,9},{9,10},{10,1... | collective-permute-start | bytes 6584 | tf_op jit(solution)/shard_map/ppermute | solution.py:14
  122.2 15.4 %copy-start.6 = (f32[137,130]{0,1:T(8,128)S(1)}, f32[137,130]{0,1:T(8,128)}, u32[]{:S(2)}) copy-start(f32[137,130]{0,1:T(8,128)} %get-tuple-element.28) | copy-start | bytes 213724
  135.6 8.1 %collective-permute-start.16 = (f32[4,137,1]{2,1,0:T(8,128)}, f32[4,137,1]{2,1,0:T(8,128)S(1)}, u32[]{:S(2)}, u32[]{:S(2)}) collective-permute-start(f32[4,137,1]{2,1,0:T(8,128)} %get-tuple-element.49), channel_id=1, source_target_pairs={{1,0},{2,1},{3,2},{0,3},{5,4},{6,5},{7,6},{4,7},{9,8},{10,9},{11,1... | collective-permute-start | bytes 6584 | tf_op jit(solution)/shard_map/ppermute | solution.py:15
  136.8 14.1 %collective-permute-start.17 = (f32[4,137,1]{2,1,0:T(8,128)}, f32[4,137,1]{2,1,0:T(8,128)S(1)}, u32[]{:S(2)}, u32[]{:S(2)}) collective-permute-start(f32[4,137,1]{2,1,0:T(8,128)} %get-tuple-element.50), channel_id=1, source_target_pairs={{0,1},{1,2},{2,3},{3,0},{4,5},{5,6},{6,7},{7,4},{8,9},{9,10},{10,1... | collective-permute-start | bytes 6584 | tf_op jit(solution)/shard_map/ppermute | solution.py:14
  151.4 15.6 %collective-permute-start.18 = (f32[4,137,1]{2,1,0:T(8,128)S(1)}, f32[4,137,1]{2,1,0:T(8,128)S(1)}, u32[]{:S(2)}, u32[]{:S(2)}) collective-permute-start(f32[4,137,1]{2,1,0:T(8,128)S(1)} %get-tuple-element.47), channel_id=1, source_target_pairs={{1,0},{2,1},{3,2},{0,3},{5,4},{6,5},{7,6},{4,7},{9,8},{10,9},{11,1... | collective-permute-start | bytes 6584 | tf_op jit(solution)/shard_map/ppermute | solution.py:15
  151.7 15.2 %collective-permute-start.19 = (f32[4,137,1]{2,1,0:T(8,128)S(1)}, f32[4,137,1]{2,1,0:T(8,128)S(1)}, u32[]{:S(2)}, u32[]{:S(2)}) collective-permute-start(f32[4,137,1]{2,1,0:T(8,128)S(1)} %get-tuple-element.48), channel_id=1, source_target_pairs={{0,1},{1,2},{2,3},{3,0},{4,5},{5,6},{6,7},{7,4},{8,9},{9,10},{10,1... | collective-permute-start | bytes 6584 | tf_op jit(solution)/shard_map/ppermute | solution.py:14
  153.4 13.5 %all-to-all-start.3 = ((f32[1,1,4,128]{3,1,0,2:T(1,128)}), f32[1,1,4,128]{3,1,0,2:T(1,128)S(1)}, u32[]{:S(2)}, u32[]{:S(2)}) async-start(f32[1,1,4,128]{3,1,0,2:T(1,128)} %bitcast.58), calls=%async_computation.3 | async-start | bytes 4096 | tf_op jit(solution)/shard_map/all_to_all | solution.py:89
where the time goes:
time: 221 us
  waiting for transfers between devices  67.2 us (30%)
  blocking collectives  48.6 us (22%)
  local copies, waits for them, and re-layouts  41.5 us (19%)
  starting transfers between devices  40.5 us (18%)
  other arithmetic  18.9 us (9%)
  between operations  4 us (2%)
    psum x1, blocking collectives, on_device(): cost, norm = lax.psum((cost_part, norm_part), ('tm', 'space'))  48.6 us
    ppermute x9, waiting for transfers between devices, padded_2(): before = lax.ppermute(last, axis, up)  27.5 us
    gather x8, local copies, waits for them, and re-layouts, on_device(): seen = weight * line[flat] + (1.0 - weight) * line[flat + 1]  25.1 us
    ppermute x9, waiting for transfers between devices, padded_2(): after = lax.ppermute(initial, axis, down)  19 us
    ppermute x9, starting transfers between devices, padded_2(): before = lax.ppermute(last, axis, up)  12.2 us
    ppermute x9, starting transfers between devices, padded_2(): after = lax.ppermute(initial, axis, down)  10.8 us
    all_to_all x1, waiting for transfers between devices, on_device(): lax.all_to_all(departed[None, None], 'space', split_axis=2, concat_axis=2...  10 us
    all_to_all x1, waiting for transfers between devices, on_device(): lax.all_to_all(obs_code, 'space', split_axis=2, concat_axis=2, tiled=True)  8.22 us
  transfers between devices with their start and end apart: 24, of which 12 were waited for; matrix products, arithmetic and copies ran while one was open for 19% of the time, Pallas kernels for 0%

commit v1 on v0

--- a/solution.py
+++ b/solution.py
@@ -84,7 +84,7 @@
     gradient = weighted_own + lam
     cost_part = 0.5 * (jump_part + jnp.sum(pushed * departed))
     norm_part = jnp.sum(gradient * gradient)
-    cost, norm = lax.psum((cost_part, norm_part), ("tm", "space"))
+    cost, norm = lax.psum(lax.psum((cost_part, norm_part), "space"), "tm")
     renewed = increment - cost / norm * gradient[None]
     returned = lax.all_to_all(
         departed[None, None], "space", split_axis=2, concat_axis=2, tiled=True

time: 221 us -> 203 us (0.919)
  blocking collectives: 48.6 us -> 30 us
    psum x1 -> x2, blocking collectives: 48.6 us -> 30 us  [on_device(): cost, norm = lax.psum(lax.psum((cost_part, norm_part), 'space'), 'tm')]
  transfers between devices with their start and end apart: 24 -> 24, of which waited for: 12 -> 12; matrix products, arithmetic and copies ran while one was open for 19% -> 21% of each run, Pallas kernels for 0% -> 0%
where the time goes in v1:
time: 203 us; the launch traced here: 202 us
  waiting for transfers between devices  67.2 us (33%)
  local copies, waits for them, and re-layouts  41.5 us (20%)
  starting transfers between devices  40.5 us (20%)
  blocking collectives  30 us (15%)
  other arithmetic  18.9 us (9%)
  between operations  3.95 us (2%)
    psum x2, blocking collectives, on_device(): cost, norm = lax.psum(lax.psum((cost_part, norm_part), 'space'), 'tm')  30 us
    ppermute x9, waiting for transfers between devices, padded_2(): before = lax.ppermute(last, axis, up)  27.5 us
    gather x8, local copies, waits for them, and re-layouts, on_device(): seen = weight * line[flat] + (1.0 - weight) * line[flat + 1]  25.1 us
    ppermute x9, waiting for transfers between devices, padded_2(): after = lax.ppermute(initial, axis, down)  19 us
    ppermute x9, starting transfers between devices, padded_2(): before = lax.ppermute(last, axis, up)  12.2 us
    ppermute x9, starting transfers between devices, padded_2(): after = lax.ppermute(initial, axis, down)  10.8 us
    all_to_all x1, waiting for transfers between devices, on_device(): lax.all_to_all(departed[None, None], 'space', split_axis=2, concat_axis=2...  10 us
    all_to_all x1, waiting for transfers between devices, on_device(): lax.all_to_all(obs_code, 'space', split_axis=2, concat_axis=2, tiled=True)  8.22 us
  transfers between devices with their start and end apart: 24, of which 12 were waited for; matrix products, arithmetic and copies ran while one was open for 21% of the time, Pallas kernels for 0%

profile of v1, /device:TPU:0, one launch (start us, length us, event | category | flops | bytes accessed | tf_op | source)
XLA Modules:
  0.0 201.9 jit_solution(11366981946119428635)
XLA Ops:
  0.6 1.3 copy.83
  1.9 5.2 %all-to-all-start.1 = ((s32[1,1,4]{1,0,2:T(1,128)}), s32[1,1,4]{1,0,2:T(1,128)S(1)}, u32[]{:S(2)}, u32[]{:S(2)}) async-start(s32[1,1,4]{1,0,2:T(1,128)} %copy.83), calls=%async_computation.1 | async-start | bytes 4096 | tf_op jit(solution)/shard_map/all_to_all | solution.py:36
  7.1 1.2 copy.68
  8.3 2.1 %collective-permute-start = (f32[4,137,1]{1,2,0:T(1,128)S(1)}, f32[4,137,1]{1,2,0:T(1,128)S(1)}, u32[]{:S(2)}, u32[]{:S(2)}) collective-permute-start(f32[4,137,1]{1,2,0:T(1,128)S(1)} %get-tuple-element.47), channel_id=1, source_target_pairs={{0,1},{1,2},{2,3},{3,0},{4,5},{5,6},{6,7},{7,4},{8,9},{9,10},{10,1... | collective-permute-start | bytes 6584 | tf_op jit(solution)/shard_map/ppermute | solution.py:14
  13.2 1.1 collective-permute-start.2
  14.3 1.9 collective-permute-start.3
  16.2 3.2 %all-to-all-start.2 = ((s32[1,1,4,128]{3,1,0,2:T(1,128)}), s32[1,1,4,128]{3,1,0,2:T(1,128)S(1)}, u32[]{:S(2)}, u32[]{:S(2)}) async-start(s32[1,1,4,128]{3,1,0,2:T(1,128)} %bitcast.16), calls=%async_computation.2 | async-start | bytes 4096 | tf_op jit(solution)/shard_map/all_to_all | solution.py:34
  20.7 8.2 %all-to-all-done.2 = s32[1,1,4,128]{3,1,0,2:T(1,128)S(1)} async-done(((s32[1,1,4,128]{3,1,0,2:T(1,128)}), s32[1,1,4,128]{3,1,0,2:T(1,128)S(1)}, u32[]{:S(2)}, u32[]{:S(2)}) %all-to-all-start.2) | async-done | bytes 2080 | tf_op jit(solution)/shard_map/all_to_all | solution.py:34
  28.9 3.2 %all-to-all-start = ((f32[1,1,4,3,128]{4,3,1,0,2:T(4,128)}), f32[1,1,4,3,128]{4,3,1,0,2:T(4,128)S(1)}, u32[]{:S(2)}, u32[]{:S(2)}) async-start(f32[1,1,4,3,128]{4,3,1,0,2:T(4,128)} %copy.81), calls=%async_computation | async-start | bytes 16384 | tf_op jit(solution)/shard_map/all_to_all | solution.py:35
  32.7 1.3 fusion.35
  34.1 2.0 %collective-permute-start.4 = (f32[4,137,1]{2,1,0:T(8,128)S(1)}, f32[4,137,1]{2,1,0:T(8,128)S(1)}, u32[]{:S(2)}, u32[]{:S(2)}) collective-permute-start(f32[4,137,1]{2,1,0:T(8,128)S(1)} %get-tuple-element.61), channel_id=1, source_target_pairs={{0,1},{1,2},{2,3},{3,0},{4,5},{5,6},{6,7},{7,4},{8,9},{9,10},{10,1... | collective-permute-start | bytes 6584 | tf_op jit(solution)/shard_map/ppermute | solution.py:14
  37.3 7.6 %collective-permute-done.4 = f32[4,137,1]{2,1,0:T(8,128)S(1)} collective-permute-done((f32[4,137,1]{2,1,0:T(8,128)S(1)}, f32[4,137,1]{2,1,0:T(8,128)S(1)}, u32[]{:S(2)}, u32[]{:S(2)}) %collective-permute-start.4) | collective-permute-done | bytes 2224 | tf_op jit(solution)/shard_map/ppermute | solution.py:14
  44.9 3.5 %collective-permute-done.5 = f32[4,137,1]{2,1,0:T(8,128)} collective-permute-done((f32[4,137,1]{2,1,0:T(8,128)S(1)}, f32[4,137,1]{2,1,0:T(8,128)}, u32[]{:S(2)}, u32[]{:S(2)}) %collective-permute-start.5) | collective-permute-done | bytes 2224 | tf_op jit(solution)/shard_map/ppermute | solution.py:15
  48.4 1.3 fusion.31
  50.6 1.5 collective-permute-start.6
  52.1 1.5 collective-permute-start.7
  54.0 3.1 %gather_fusion.7 = f32[512]{0:T(512)S(1)} fusion(f32[70144]{0:T(1024)S(1)} %reshape.355, s32[1024]{0:T(1024)S(1)} %get-tuple-element.74), kind=kCustom, calls=%fused_computation.7 | custom fusion | bytes 6144 | tf_op jit(solution)/shard_map/gather | solution.py:61
  57.1 3.1 %gather_fusion.6 = f32[512]{0:T(512)S(1)} fusion(f32[70144]{0:T(1024)S(1)} %reshape.355, s32[1024]{0:T(1024)S(1)} %get-tuple-element.75), kind=kCustom, calls=%fused_computation.6 | custom fusion | bytes 6144 | tf_op jit(solution)/shard_map/gather | solution.py:61
  60.3 3.1 %gather_fusion.5 = f32[512]{0:T(512)S(1)} fusion(f32[70144]{0:T(1024)S(1)} %reshape.354, s32[1024]{0:T(1024)S(1)} %get-tuple-element.74), kind=kCustom, calls=%fused_computation.5 | custom fusion | bytes 6144 | tf_op jit(solution)/shard_map/gather | solution.py:61
  63.4 3.1 %gather_fusion.4 = f32[512]{0:T(512)S(1)} fusion(f32[70144]{0:T(1024)S(1)} %reshape.354, s32[1024]{0:T(1024)S(1)} %get-tuple-element.75), kind=kCustom, calls=%fused_computation.4 | custom fusion | bytes 6144 | tf_op jit(solution)/shard_map/gather | solution.py:61
  66.6 1.3 fusion.27
  68.6 2.4 %collective-permute-start.9 = (f32[4,137,1]{2,1,0:T(8,128)S(1)}, f32[4,137,1]{2,1,0:T(8,128)S(1)}, u32[]{:S(2)}, u32[]{:S(2)}) collective-permute-start(f32[4,137,1]{2,1,0:T(8,128)S(1)} %get-tuple-element.58), channel_id=1, source_target_pairs={{1,0},{2,1},{3,2},{0,3},{5,4},{6,5},{7,6},{4,7},{9,8},{10,9},{11,1... | collective-permute-start | bytes 6584 | tf_op jit(solution)/shard_map/ppermute | solution.py:15
  71.0 3.1 %gather_fusion.3 = f32[512]{0:T(512)S(1)} fusion(f32[70144]{0:T(1024)S(1)} %reshape.353, s32[1024]{0:T(1024)S(1)} %get-tuple-element.74), kind=kCustom, calls=%fused_computation.3 | custom fusion | bytes 6144 | tf_op jit(solution)/shard_map/gather | solution.py:61
  74.2 3.1 %gather_fusion.2 = f32[512]{0:T(512)S(1)} fusion(f32[70144]{0:T(1024)S(1)} %reshape.353, s32[1024]{0:T(1024)S(1)} %get-tuple-element.75), kind=kCustom, calls=%fused_computation.2 | custom fusion | bytes 6144 | tf_op jit(solution)/shard_map/gather | solution.py:61
  77.4 1.9 collective-permute-done.9
  79.6 3.1 %gather_fusion.1 = f32[512]{0:T(512)S(1)} fusion(f32[70144]{0:T(1024)S(1)} %reshape.352, s32[1024]{0:T(1024)S(1)} %get-tuple-element.74), kind=kCustom, calls=%fused_computation.1 | custom fusion | bytes 6144 | tf_op jit(solution)/shard_map/gather | solution.py:61
  82.8 3.1 %gather_fusion = f32[512]{0:T(512)S(1)} fusion(f32[70144]{0:T(1024)S(1)} %reshape.352, s32[1024]{0:T(1024)S(1)} %get-tuple-element.75), kind=kCustom, calls=%fused_computation | custom fusion | bytes 6144 | tf_op jit(solution)/shard_map/gather | solution.py:61
  85.9 1.3 collective-permute-start.10
  88.7 3.5 %scatter_custom_fusion = f32[280576]{0:T(1024)S(1)} fusion(s32[512]{0:T(512)S(1)} %fusion.42, f32[512]{0:T(512)S(1)} %get-tuple-element.69, f32[]{:T(128)} %constant.16.clone.1), kind=kCustom, calls=%fused_computation.10 | custom fusion | flops 512 | bytes 1122308 | tf_op jit(solution)/shard_map/scatter-add | solution.py:72
  92.2 3.7 %scatter_fusion = f32[280576]{0:T(1024)S(1)} fusion(f32[280576]{0:T(1024)S(1)} %scatter_custom_fusion, s32[512]{0:T(512)S(1)} %get-tuple-element.72, f32[512]{0:T(512)S(1)} %get-tuple-element.68), kind=kCustom, calls=%fused_computation.9 | custom fusion | flops 512 | bytes 8192 | tf_op jit(solution)/shard_map/scatter-add | solution.py:72
  96.8 1.3 collective-permute-start.11
  100.0 2.4 %collective-permute-done.11 = f32[4,137,128]{2,1,0:T(8,128)} collective-permute-done((f32[4,137,128]{2,1,0:T(8,128)}, f32[4,137,128]{2,1,0:T(8,128)}, u32[]{:S(2)}, u32[]{:S(2)}) %collective-permute-start.11) | collective-permute-done | bytes 280608 | tf_op jit(solution)/shard_map/ppermute | solution.py:23
  104.4 1.2 collective-permute-start.12
  108.4 3.0 %collective-permute-done.12 = f32[4,137,1]{2,1,0:T(8,128)} collective-permute-done((f32[4,137,1]{2,1,0:T(8,128)}, f32[4,137,1]{2,1,0:T(8,128)}, u32[]{:S(2)}, u32[]{:S(2)}) %collective-permute-start.12) | collective-permute-done | bytes 2224 | tf_op jit(solution)/shard_map/ppermute | solution.py:15
  111.4 6.2 %collective-permute-done.13 = f32[4,137,1]{2,1,0:T(8,128)} collective-permute-done((f32[4,137,1]{2,1,0:T(8,128)}, f32[4,137,1]{2,1,0:T(8,128)}, u32[]{:S(2)}, u32[]{:S(2)}) %collective-permute-start.13) | collective-permute-done | bytes 2224 | tf_op jit(solution)/shard_map/ppermute | solution.py:14
  117.6 1.4 fusion.19
  120.2 1.7 collective-permute-start.15
  122.2 4.7 %collective-permute-done.14 = f32[4,137,1]{2,1,0:T(8,128)S(1)} collective-permute-done((f32[4,137,1]{2,1,0:T(8,128)}, f32[4,137,1]{2,1,0:T(8,128)S(1)}, u32[]{:S(2)}, u32[]{:S(2)}) %collective-permute-start.14) | collective-permute-done | bytes 2224 | tf_op jit(solution)/shard_map/ppermute | solution.py:15
  127.0 6.5 %collective-permute-done.15 = f32[4,137,1]{2,1,0:T(8,128)} collective-permute-done((f32[4,137,1]{2,1,0:T(8,128)}, f32[4,137,1]{2,1,0:T(8,128)}, u32[]{:S(2)}, u32[]{:S(2)}) %collective-permute-start.15) | collective-permute-done | bytes 2224 | tf_op jit(solution)/shard_map/ppermute | solution.py:14
  133.4 1.3 fusion.14
  135.6 1.2 collective-permute-start.16
  137.9 5.8 %collective-permute-done.16 = f32[4,137,1]{2,1,0:T(8,128)S(1)} collective-permute-done((f32[4,137,1]{2,1,0:T(8,128)}, f32[4,137,1]{2,1,0:T(8,128)S(1)}, u32[]{:S(2)}, u32[]{:S(2)}) %collective-permute-start.16) | collective-permute-done | bytes 2224 | tf_op jit(solution)/shard_map/ppermute | solution.py:15
  143.7 7.2 %collective-permute-done.17 = f32[4,137,1]{2,1,0:T(8,128)S(1)} collective-permute-done((f32[4,137,1]{2,1,0:T(8,128)}, f32[4,137,1]{2,1,0:T(8,128)S(1)}, u32[]{:S(2)}, u32[]{:S(2)}) %collective-permute-start.17) | collective-permute-done | bytes 2224 | tf_op jit(solution)/shard_map/ppermute | solution.py:14
  151.7 1.7 collective-permute-start.19
  153.4 3.2 %all-to-all-start.3 = ((f32[1,1,4,128]{3,1,0,2:T(1,128)}), f32[1,1,4,128]{3,1,0,2:T(1,128)S(1)}, u32[]{:S(2)}, u32[]{:S(2)}) async-start(f32[1,1,4,128]{3,1,0,2:T(1,128)} %bitcast.58), calls=%async_computation.3 | async-start | bytes 4096 | tf_op jit(solution)/shard_map/all_to_all | solution.py:89
  156.9 10.0 %all-to-all-done.3 = f32[1,1,4,128]{3,1,0,2:T(1,128)S(1)} async-done(((f32[1,1,4,128]{3,1,0,2:T(1,128)}), f32[1,1,4,128]{3,1,0,2:T(1,128)S(1)}, u32[]{:S(2)}, u32[]{:S(2)}) %all-to-all-start.3) | async-done | bytes 2080 | tf_op jit(solution)/shard_map/all_to_all | solution.py:89
  169.2 9.3 %all-reduce.1 = (f32[]{:T(128)}, f32[]{:T(128)}) all-reduce(f32[]{:T(128)S(6)} %mul.422, f32[]{:T(128)} %get-tuple-element.14), channel_id=1, replica_groups=mesh['tm'=8,'space'=4] {'space'}, use_global_device_ids=true, to_apply=%region_2.3 | all-reduce | flops 2 | bytes 16 | tf_op jit(solution)/shard_map/psum | solution.py:87
  178.5 20.6 %all-reduce = (f32[]{:T(128)}, f32[]{:T(128)}) all-reduce(f32[]{:T(128)} %get-tuple-element.10, f32[]{:T(128)} %get-tuple-element.11), channel_id=1, replica_groups=mesh['tm'=8,'space'=4] {'tm'}, use_global_device_ids=true, to_apply=%region_3.4 | all-reduce | flops 2 | bytes 16 | tf_op jit(solution)/shard_map/psum | solution.py:87
  (110 shorter events, 24.0 us)
Async XLA Ops:
  1.9 14.2 %all-to-all-start.1 = ((s32[1,1,4]{1,0,2:T(1,128)}), s32[1,1,4]{1,0,2:T(1,128)S(1)}, u32[]{:S(2)}, u32[]{:S(2)}) async-start(s32[1,1,4]{1,0,2:T(1,128)} %copy.83), calls=%async_computation.1 | async-start | bytes 4096 | tf_op jit(solution)/shard_map/all_to_all | solution.py:36
  8.3 23.9 %collective-permute-start = (f32[4,137,1]{1,2,0:T(1,128)S(1)}, f32[4,137,1]{1,2,0:T(1,128)S(1)}, u32[]{:S(2)}, u32[]{:S(2)}) collective-permute-start(f32[4,137,1]{1,2,0:T(1,128)S(1)} %get-tuple-element.47), channel_id=1, source_target_pairs={{0,1},{1,2},{2,3},{3,0},{4,5},{5,6},{6,7},{7,4},{8,9},{9,10},{10,1... | collective-permute-start | bytes 6584 | tf_op jit(solution)/shard_map/ppermute | solution.py:14
  10.4 21.8 %collective-permute-start.1 = (f32[4,137,1]{1,2,0:T(1,128)S(1)}, f32[4,137,1]{1,2,0:T(1,128)S(1)}, u32[]{:S(2)}, u32[]{:S(2)}) collective-permute-start(f32[4,137,1]{1,2,0:T(1,128)S(1)} %get-tuple-element.48), channel_id=1, source_target_pairs={{1,0},{2,1},{3,2},{0,3},{5,4},{6,5},{7,6},{4,7},{9,8},{10,9},{11,1... | collective-permute-start | bytes 6584 | tf_op jit(solution)/shard_map/ppermute | solution.py:15
  13.2 6.3 %copy-start.10 = (f32[1,1,4,3,128]{4,2,3,1,0:T(4,128)S(1)}, f32[1,1,4,3,128]{4,2,3,1,0:T(4,128)}, u32[]{:S(2)}) copy-start(f32[1,1,4,3,128]{4,2,3,1,0:T(4,128)} %param.10) | copy-start | bytes 18436
  13.2 19.4 %collective-permute-start.2 = (f32[4,137,1]{2,1,0:T(8,128)}, f32[4,137,1]{2,1,0:T(8,128)S(1)}, u32[]{:S(2)}, u32[]{:S(2)}) collective-permute-start(f32[4,137,1]{2,1,0:T(8,128)} %get-tuple-element.63), channel_id=1, source_target_pairs={{0,1},{1,2},{2,3},{3,0},{4,5},{5,6},{6,7},{7,4},{8,9},{9,10},{10,1... | collective-permute-start | bytes 6584 | tf_op jit(solution)/shard_map/ppermute | solution.py:14
  14.3 18.4 %collective-permute-start.3 = (f32[4,137,1]{2,1,0:T(8,128)}, f32[4,137,1]{2,1,0:T(8,128)}, u32[]{:S(2)}, u32[]{:S(2)}) collective-permute-start(f32[4,137,1]{2,1,0:T(8,128)} %get-tuple-element.64), channel_id=1, source_target_pairs={{1,0},{2,1},{3,2},{0,3},{5,4},{6,5},{7,6},{4,7},{9,8},{10,9},{11,1... | collective-permute-start | bytes 6584 | tf_op jit(solution)/shard_map/ppermute | solution.py:15
  16.2 12.7 %all-to-all-start.2 = ((s32[1,1,4,128]{3,1,0,2:T(1,128)}), s32[1,1,4,128]{3,1,0,2:T(1,128)S(1)}, u32[]{:S(2)}, u32[]{:S(2)}) async-start(s32[1,1,4,128]{3,1,0,2:T(1,128)} %bitcast.16), calls=%async_computation.2 | async-start | bytes 4096 | tf_op jit(solution)/shard_map/all_to_all | solution.py:34
  20.2 59.1 %copy-start.4 = (f32[137,128]{1,0:T(8,128)}, f32[137,128]{1,0:T(8,128)S(1)}, u32[]{:S(2)}) copy-start(f32[137,128]{1,0:T(8,128)S(1)} %copy.69) | copy-start | bytes 210436
  20.5 46.1 %copy-start.2 = (f32[137,128]{1,0:T(8,128)}, f32[137,128]{1,0:T(8,128)S(1)}, u32[]{:S(2)}) copy-start(f32[137,128]{1,0:T(8,128)S(1)} %copy.70) | copy-start | bytes 210436
  28.9 42.1 %all-to-all-start = ((f32[1,1,4,3,128]{4,3,1,0,2:T(4,128)}), f32[1,1,4,3,128]{4,3,1,0,2:T(4,128)S(1)}, u32[]{:S(2)}, u32[]{:S(2)}) async-start(f32[1,1,4,3,128]{4,3,1,0,2:T(4,128)} %copy.81), calls=%async_computation | async-start | bytes 16384 | tf_op jit(solution)/shard_map/all_to_all | solution.py:35
  34.1 10.8 %collective-permute-start.4 = (f32[4,137,1]{2,1,0:T(8,128)S(1)}, f32[4,137,1]{2,1,0:T(8,128)S(1)}, u32[]{:S(2)}, u32[]{:S(2)}) collective-permute-start(f32[4,137,1]{2,1,0:T(8,128)S(1)} %get-tuple-element.61), channel_id=1, source_target_pairs={{0,1},{1,2},{2,3},{3,0},{4,5},{5,6},{6,7},{7,4},{8,9},{9,10},{10,1... | collective-permute-start | bytes 6584 | tf_op jit(solution)/shard_map/ppermute | solution.py:14
  36.1 12.3 %collective-permute-start.5 = (f32[4,137,1]{2,1,0:T(8,128)S(1)}, f32[4,137,1]{2,1,0:T(8,128)}, u32[]{:S(2)}, u32[]{:S(2)}) collective-permute-start(f32[4,137,1]{2,1,0:T(8,128)S(1)} %get-tuple-element.62), channel_id=1, source_target_pairs={{1,0},{2,1},{3,2},{0,3},{5,4},{6,5},{7,6},{4,7},{9,8},{10,9},{11,1... | collective-permute-start | bytes 6584 | tf_op jit(solution)/shard_map/ppermute | solution.py:15
  50.6 16.0 %collective-permute-start.6 = (f32[4,137,1]{2,1,0:T(8,128)}, f32[4,137,1]{2,1,0:T(8,128)S(1)}, u32[]{:S(2)}, u32[]{:S(2)}) collective-permute-start(f32[4,137,1]{2,1,0:T(8,128)} %get-tuple-element.59), channel_id=1, source_target_pairs={{0,1},{1,2},{2,3},{3,0},{4,5},{5,6},{6,7},{7,4},{8,9},{9,10},{10,1... | collective-permute-start | bytes 6584 | tf_op jit(solution)/shard_map/ppermute | solution.py:14
  52.1 14.5 %collective-permute-start.7 = (f32[4,137,1]{2,1,0:T(8,128)}, f32[4,137,1]{2,1,0:T(8,128)}, u32[]{:S(2)}, u32[]{:S(2)}) collective-permute-start(f32[4,137,1]{2,1,0:T(8,128)} %get-tuple-element.60), channel_id=1, source_target_pairs={{1,0},{2,1},{3,2},{0,3},{5,4},{6,5},{7,6},{4,7},{9,8},{10,9},{11,1... | collective-permute-start | bytes 6584 | tf_op jit(solution)/shard_map/ppermute | solution.py:15
  68.0 9.3 %collective-permute-start.8 = (f32[4,137,1]{2,1,0:T(8,128)S(1)}, f32[4,137,1]{2,1,0:T(8,128)S(1)}, u32[]{:S(2)}, u32[]{:S(2)}) collective-permute-start(f32[4,137,1]{2,1,0:T(8,128)S(1)} %get-tuple-element.57), channel_id=1, source_target_pairs={{0,1},{1,2},{2,3},{3,0},{4,5},{5,6},{6,7},{7,4},{8,9},{9,10},{10,1... | collective-permute-start | bytes 6584 | tf_op jit(solution)/shard_map/ppermute | solution.py:14
  68.6 10.7 %collective-permute-start.9 = (f32[4,137,1]{2,1,0:T(8,128)S(1)}, f32[4,137,1]{2,1,0:T(8,128)S(1)}, u32[]{:S(2)}, u32[]{:S(2)}) collective-permute-start(f32[4,137,1]{2,1,0:T(8,128)S(1)} %get-tuple-element.58), channel_id=1, source_target_pairs={{1,0},{2,1},{3,2},{0,3},{5,4},{6,5},{7,6},{4,7},{9,8},{10,9},{11,1... | collective-permute-start | bytes 6584 | tf_op jit(solution)/shard_map/ppermute | solution.py:15
  85.9 10.0 %collective-permute-start.10 = (f32[4,137,128]{2,1,0:T(8,128)S(1)}, f32[4,137,128]{2,1,0:T(8,128)S(1)}, u32[]{:S(2)}, u32[]{:S(2)}) collective-permute-start(f32[4,137,128]{2,1,0:T(8,128)S(1)} %fusion.23), channel_id=1, source_target_pairs={{0,4},{4,8},{8,12},{12,16},{16,20},{20,24},{24,28},{1,5},{5,9},{9,... | collective-permute-start | bytes 841736 | tf_op jit(solution)/shard_map/ppermute | solution.py:23
  92.2 3.7 %copy-start = (f32[1,4,137,128]{3,1,2,0:T(4,128)S(1)}, f32[1,4,137,128]{3,1,2,0:T(4,128)}, u32[]{:S(2)}) copy-start(f32[1,4,137,128]{3,1,2,0:T(4,128)} %param.6) | copy-start | bytes 841732
  92.2 3.7 %copy-start.9 = (f32[4,137]{1,0:T(4,128)S(1)}, f32[4,137]{1,0:T(4,128)}, u32[]{:S(2)}) copy-start(f32[4,137]{1,0:T(4,128)} %param.8) | copy-start | bytes 6580
  96.8 5.6 %collective-permute-start.11 = (f32[4,137,128]{2,1,0:T(8,128)}, f32[4,137,128]{2,1,0:T(8,128)}, u32[]{:S(2)}, u32[]{:S(2)}) collective-permute-start(f32[4,137,128]{2,1,0:T(8,128)} %broadcast_multiply_fusion), channel_id=1, source_target_pairs={{4,0},{8,4},{12,8},{16,12},{20,16},{24,20},{28,24},{5,1},{9,5},{13... | collective-permute-start | bytes 841736 | tf_op jit(solution)/shard_map/ppermute | solution.py:23
  104.4 7.0 %collective-permute-start.12 = (f32[4,137,1]{2,1,0:T(8,128)}, f32[4,137,1]{2,1,0:T(8,128)}, u32[]{:S(2)}, u32[]{:S(2)}) collective-permute-start(f32[4,137,1]{2,1,0:T(8,128)} %get-tuple-element.55), channel_id=1, source_target_pairs={{1,0},{2,1},{3,2},{0,3},{5,4},{6,5},{7,6},{4,7},{9,8},{10,9},{11,1... | collective-permute-start | bytes 6584 | tf_op jit(solution)/shard_map/ppermute | solution.py:15
  105.6 2.8 %copy-start.1 = (f32[70144]{0:T(1024)S(1)}, f32[70144]{0:T(1024)}, u32[]{:S(2)}) copy-start(f32[70144]{0:T(1024)} %get-tuple-element.23) | copy-start | bytes 841732
  105.6 12.0 %collective-permute-start.13 = (f32[4,137,1]{2,1,0:T(8,128)}, f32[4,137,1]{2,1,0:T(8,128)}, u32[]{:S(2)}, u32[]{:S(2)}) collective-permute-start(f32[4,137,1]{2,1,0:T(8,128)} %get-tuple-element.56), channel_id=1, source_target_pairs={{0,1},{1,2},{2,3},{3,0},{4,5},{5,6},{6,7},{7,4},{8,9},{9,10},{10,1... | collective-permute-start | bytes 6584 | tf_op jit(solution)/shard_map/ppermute | solution.py:14
  107.2 10.4 %copy-start.5 = (f32[137,128]{1,0:T(8,128)S(1)}, f32[137,128]{1,0:T(8,128)}, u32[]{:S(2)}) copy-start(f32[137,128]{1,0:T(8,128)} %copy-done.4) | copy-start | bytes 210436
  108.4 13.5 %copy-start.8 = (f32[137,130]{0,1:T(8,128)S(1)}, f32[137,130]{0,1:T(8,128)}, u32[]{:S(2)}) copy-start(f32[137,130]{0,1:T(8,128)} %get-tuple-element.31) | copy-start | bytes 213724
  119.0 3.1 %copy-start.7 = (f32[137,130]{0,1:T(8,128)S(1)}, f32[137,130]{0,1:T(8,128)}, u32[]{:S(2)}) copy-start(f32[137,130]{0,1:T(8,128)} %get-tuple-element.77) | copy-start | bytes 213724
  119.0 14.4 %copy-start.3 = (f32[137,128]{1,0:T(8,128)S(1)}, f32[137,128]{1,0:T(8,128)}, u32[]{:S(2)}) copy-start(f32[137,128]{1,0:T(8,128)} %copy-done.2) | copy-start | bytes 210436
  119.9 7.0 %collective-permute-start.14 = (f32[4,137,1]{2,1,0:T(8,128)}, f32[4,137,1]{2,1,0:T(8,128)S(1)}, u32[]{:S(2)}, u32[]{:S(2)}) collective-permute-start(f32[4,137,1]{2,1,0:T(8,128)} %get-tuple-element.53), channel_id=1, source_target_pairs={{1,0},{2,1},{3,2},{0,3},{5,4},{6,5},{7,6},{4,7},{9,8},{10,9},{11,1... | collective-permute-start | bytes 6584 | tf_op jit(solution)/shard_map/ppermute | solution.py:15
  120.2 13.2 %collective-permute-start.15 = (f32[4,137,1]{2,1,0:T(8,128)}, f32[4,137,1]{2,1,0:T(8,128)}, u32[]{:S(2)}, u32[]{:S(2)}) collective-permute-start(f32[4,137,1]{2,1,0:T(8,128)} %get-tuple-element.54), channel_id=1, source_target_pairs={{0,1},{1,2},{2,3},{3,0},{4,5},{5,6},{6,7},{7,4},{8,9},{9,10},{10,1... | collective-permute-start | bytes 6584 | tf_op jit(solution)/shard_map/ppermute | solution.py:14
  122.2 15.4 %copy-start.6 = (f32[137,130]{0,1:T(8,128)S(1)}, f32[137,130]{0,1:T(8,128)}, u32[]{:S(2)}) copy-start(f32[137,130]{0,1:T(8,128)} %get-tuple-element.30) | copy-start | bytes 213724
  135.6 8.1 %collective-permute-start.16 = (f32[4,137,1]{2,1,0:T(8,128)}, f32[4,137,1]{2,1,0:T(8,128)S(1)}, u32[]{:S(2)}, u32[]{:S(2)}) collective-permute-start(f32[4,137,1]{2,1,0:T(8,128)} %get-tuple-element.51), channel_id=1, source_target_pairs={{1,0},{2,1},{3,2},{0,3},{5,4},{6,5},{7,6},{4,7},{9,8},{10,9},{11,1... | collective-permute-start | bytes 6584 | tf_op jit(solution)/shard_map/ppermute | solution.py:15
  136.8 14.1 %collective-permute-start.17 = (f32[4,137,1]{2,1,0:T(8,128)}, f32[4,137,1]{2,1,0:T(8,128)S(1)}, u32[]{:S(2)}, u32[]{:S(2)}) collective-permute-start(f32[4,137,1]{2,1,0:T(8,128)} %get-tuple-element.52), channel_id=1, source_target_pairs={{0,1},{1,2},{2,3},{3,0},{4,5},{5,6},{6,7},{7,4},{8,9},{9,10},{10,1... | collective-permute-start | bytes 6584 | tf_op jit(solution)/shard_map/ppermute | solution.py:14
  151.3 15.6 %collective-permute-start.18 = (f32[4,137,1]{2,1,0:T(8,128)S(1)}, f32[4,137,1]{2,1,0:T(8,128)S(1)}, u32[]{:S(2)}, u32[]{:S(2)}) collective-permute-start(f32[4,137,1]{2,1,0:T(8,128)S(1)} %get-tuple-element.49), channel_id=1, source_target_pairs={{1,0},{2,1},{3,2},{0,3},{5,4},{6,5},{7,6},{4,7},{9,8},{10,9},{11,1... | collective-permute-start | bytes 6584 | tf_op jit(solution)/shard_map/ppermute | solution.py:15
  151.7 15.2 %collective-permute-start.19 = (f32[4,137,1]{2,1,0:T(8,128)S(1)}, f32[4,137,1]{2,1,0:T(8,128)S(1)}, u32[]{:S(2)}, u32[]{:S(2)}) collective-permute-start(f32[4,137,1]{2,1,0:T(8,128)S(1)} %get-tuple-element.50), channel_id=1, source_target_pairs={{0,1},{1,2},{2,3},{3,0},{4,5},{5,6},{6,7},{7,4},{8,9},{9,10},{10,1... | collective-permute-start | bytes 6584 | tf_op jit(solution)/shard_map/ppermute | solution.py:14
  153.4 13.5 %all-to-all-start.3 = ((f32[1,1,4,128]{3,1,0,2:T(1,128)}), f32[1,1,4,128]{3,1,0,2:T(1,128)S(1)}, u32[]{:S(2)}, u32[]{:S(2)}) async-start(f32[1,1,4,128]{3,1,0,2:T(1,128)} %bitcast.58), calls=%async_computation.3 | async-start | bytes 4096 | tf_op jit(solution)/shard_map/all_to_all | solution.py:89
